TPU v7x, 32 devices: a whole 2x2x4 slice. The times are simulated.
32 devices in a mesh: grp: 2 (over y), gx: 4 (over z), gy: 2 (over x), gz: 2 (over core).
Axes of the slice: x: 2, y: 2, z: 4, core: 2. Of those that a mesh axis runs over, the one named last changes fastest.
Arguments:
- voltages: int32 [1024, 49152], P('gy', ('grp', 'gx', 'gz')), parts along dimension 1, may hold values from -128 to 127
Outputs:
- visibilities: bfloat16 [256, 2, 1024, 1024], P(('grp', 'gx', 'gz'), None, 'gy'), parts along dimension 0
There are 2 independent parts, one for each index of `grp`. A program takes and returns all parts, laid end to end along the dimension named above; each array names one. Nothing has to cross between parts.
All inputs are finite; a program needn't handle non-finite values.
Results may differ from a plain program's by a relative error of at most 0.0056.
Values may be sent and summed in bfloat16 or wider, within the bound.
A program may use at most 128 MiB of HBM per device.

v0:
```python
import math

import jax
import jax.numpy as jnp
from jax import lax
from jax.sharding import PartitionSpec as P

CHANS = 128
POINTS = 512
TAPS = 4


def passed_along(value, axis, by):
    peers = lax.axis_size(axis)
    pairs = [(i, i + by) for i in range(peers) if 0 <= i + by < peers]
    return lax.ppermute(value, axis, pairs)


def filter_taps(taps_count, points):
    index = jnp.arange(taps_count * points, dtype=jnp.float32)
    centre = (taps_count * points - 1) / 2.0
    window = 0.5 - 0.5 * jnp.cos(2.0 * math.pi * (index + 0.5) / (taps_count * points))
    return (
        (jnp.sinc((index - centre) / points) * window)
        .astype(jnp.float32)
        .reshape(taps_count, points)
    )


def basis_table(channels, points):
    sample = jnp.arange(points, dtype=jnp.int32)[None, :]
    channel = 64 + jnp.arange(channels, dtype=jnp.int32)[:, None]
    phase = (sample * channel % points).astype(jnp.float32) * (2.0 * math.pi / points)
    scale = 1.0 / math.sqrt(points)
    return jnp.stack([jnp.cos(phase) * scale, -jnp.sin(phase) * scale], axis=1).astype(jnp.bfloat16)


def per_device(voltages):
    inputs_here = voltages.shape[0]
    spec_here = voltages.shape[1] // POINTS
    tail = voltages[:, (spec_here - TAPS + 1) * POINTS :].astype(jnp.bfloat16)
    earlier = passed_along(tail, ("gx", "gz"), 1)
    joined = jnp.concatenate([earlier.astype(jnp.float32), voltages.astype(jnp.float32)], axis=1)
    joined = joined.reshape(inputs_here, spec_here + TAPS - 1, POINTS)
    taps = filter_taps(TAPS, POINTS)
    running = jnp.zeros((inputs_here, spec_here, POINTS), jnp.float32)
    for offset in range(TAPS):
        running = running + taps[offset][None, None, :] * joined[:, offset : offset + spec_here]
    frames = (running * (1.0 / 128.0)).astype(jnp.bfloat16)
    basis = basis_table(CHANS, POINTS)
    spectra = jnp.einsum("krn,isn->krsi", basis, frames, preferred_element_type=jnp.float32).astype(
        jnp.bfloat16
    )
    turned = lax.all_to_all(spectra, ("gx", "gz"), split_axis=0, concat_axis=2, tiled=True)
    chans_here = turned.shape[0]
    nspec_all = turned.shape[2]
    real_part = turned[:, 0]
    imag_part = turned[:, 1]
    rows_a = jnp.concatenate([real_part, imag_part], axis=1)
    rows_b = jnp.concatenate([imag_part, -real_part], axis=1)
    stacked = jnp.stack([rows_a, rows_b], axis=1)
    inverse = 1.0 / nspec_all
    piece = lax.all_gather(turned, "gy", axis=3, tiled=True)
    columns = piece.reshape(chans_here, 2 * nspec_all, piece.shape[3])
    product = jnp.einsum("cokr,ckw->corw", stacked, columns, preferred_element_type=jnp.float32)
    return (product * inverse).astype(jnp.bfloat16)


def solution(mesh):
    return jax.shard_map(
        per_device,
        mesh=mesh,
        in_specs=(P("gy", ("grp", "gx", "gz")),),
        out_specs=P(("grp", "gx", "gz"), None, "gy", None),
        check_vma=False,
    )
```

profile of v0, /device:TPU:16, one launch (start us, length us, event | category | flops | bytes accessed | tf_op | source)
XLA Modules:
  0.0 167.3 jit_solution(11663526004972213427)
XLA Ops:
  6.5 0.0 all-gather.2.cloned.1.call-start
  6.5 6.6 %copy.18 = s32[512,3072]{0,1:T(8,128)} copy(s32[512,3072]{1,0:T(8,128)} %param.1) | data formatting | bytes 12582912 | tf_op args[0]
  13.1 2.3 %slice_convert_fusion = bf16[512,1536]{0,1:T(8,128)(2,1)S(1)} fusion(s32[512,3072]{0,1:T(8,128)} %copy.18), kind=kLoop, calls=%fused_computation.11 | loop fusion | flops 786432 | bytes 4718592 | tf_op jit(solution)/shard_map/convert.2
  15.4 1.9 %collective-permute-start = (bf16[512,1536]{0,1:T(8,128)(2,1)S(1)}, bf16[512,1536]{0,1:T(8,128)(2,1)S(1)}, u32[]{:S(2)}, u32[]{:S(2)}) collective-permute-start(bf16[512,1536]{0,1:T(8,128)(2,1)S(1)} %slice_convert_fusion), channel_id=1, source_target_pairs={{0,1},{1,4},{4,5},{5,8},{8,9},{9,12},{12,13},{2,3},{3,6},{6,7},{7,... | collective-permute-start | bytes 4718600 | tf_op jit(solution)/shard_map/ppermute | solution.py:16
  17.3 3.5 %convert_element_type.42 = f32[512,3072]{0,1:T(8,128)S(1)} convert(s32[512,3072]{0,1:T(8,128)} %copy.18) | non-fusion elementwise | flops 1572864 | bytes 12582912 | tf_op jit(solution)/shard_map/convert_element_type | solution.py:43
  20.9 0.1 fusion.29
  21.0 1.2 multiply_convert_fusion.2
  22.2 14.9 %collective-permute-done = bf16[512,1536]{0,1:T(8,128)(2,1)S(1)} collective-permute-done((bf16[512,1536]{0,1:T(8,128)(2,1)S(1)}, bf16[512,1536]{0,1:T(8,128)(2,1)S(1)}, u32[]{:S(2)}, u32[]{:S(2)}) %collective-permute-start) | collective-permute-done | bytes 1572896 | tf_op jit(solution)/shard_map/ppermute | solution.py:16
  37.1 0.4 convert_element_type.41
  37.6 4.9 %pad_maximum_fusion = f32[512,4608]{0,1:T(8,128)} fusion(f32[512,3072]{0,1:T(8,128)S(1)} %convert_element_type.42, f32[512,1536]{0,1:T(8,128)S(1)} %convert_element_type.41), kind=kLoop, calls=%fused_computation.1 | loop fusion | flops 2359296 | bytes 18874368 | tf_op jit(solution)/shard_map/concatenate | solution.py:43
  42.4 10.6 %fusion.14 = bf16[128,2,6,512]{0,3,1,2:T(8,128)(2,1)S(1)} fusion(f32[512,9,512]{0,2,1:T(8,128)} %bitcast.40, f32[512]{0:T(512)S(1)} %get-tuple-element.10, f32[512]{0:T(512)S(1)} %get-tuple-element.11, f32[512]{0:T(512)S(1)} %get-tuple-element.12, f32[512]{0:T(512)S(1)} %get-tuple-element.9, bf16[128,1,512]{2,0,1:T(8,128)(2,1)S(1)} %get-tuple-element.14, ...), kind=kOutput, calls=%fused_computation.20 | convolution fusion | flops 820772864 | bytes 27009024 | tf_op jit(solution)/shard_map/krn,isn->krsi/dot_general | solution.py:51
  53.1 1.5 copy.21
  54.5 39.5 %all_to_all.18 = bf16[128,2,6,512]{3,1,2,0:T(2,128)(2,1)S(1)} all-to-all(bf16[128,2,6,512]{3,1,2,0:T(2,128)(2,1)S(1)} %copy.21), channel_id=1, replica_groups=mesh['grp'=2,'gx'=4,'gy'=2,'gz'=2] {'gx','gz'}, dimensions={0} | all-to-all | bytes 3145728 | tf_op jit(solution)/shard_map/all_to_all | solution.py:54
  94.1 0.3 copy.22
  94.4 1.3 copy.23
  95.7 0.0 all-gather.2.cloned.1.call-update
  95.7 1.5 fusion.58
  97.2 0.5 fusion.57
  97.7 0.9 copy_bitcast_fusion
  98.5 0.3 maximum_bitcast_fusion
  98.8 43.6 %all-gather.2.cloned.1.call-done = bf16[16,2,48,1024]{3,0,2,1:T(8,128)(2,1)} async-done(((bf16[16,2,48,512]{3,0,2,1:T(8,128)(2,1)}), bf16[16,2,48,1024]{3,0,2,1:T(8,128)(2,1)}) %all-gather.2.cloned.1.call-update) | async-done | bytes 3145744 | tf_op jit(solution)/shard_map/all_gather | solution.py:63
  142.5 3.6 %copy.27 = bf16[16,2,48,1024]{3,2,1,0:T(8,128)(2,1)S(1)} copy(bf16[16,2,48,1024]{3,0,2,1:T(8,128)(2,1)} %all-gather.2.cloned.1.call-done) | data formatting | bytes 6291456 | tf_op jit(solution)/shard_map/all_gather | solution.py:63
  146.1 14.3 %multiply_convert_fusion = bf16[16,2,512,1024]{3,2,1,0:T(8,128)(2,1)} fusion(bf16[16,96,1024,1]{2,1,3,0:T(8,128)(2,1)S(1)} %bitcast.37, bf16[16,1,96,512]{3,2,1,0:T(8,128)(2,1)S(1)} %get-tuple-element.8, bf16[16,1,96,512]{3,2,1,0:T(8,128)(2,1)S(1)} %get-tuple-element.7), kind=kOutput, calls=%fused_computation | convolution fusion | flops 3256352768 | bytes 39845888 | tf_op jit(solution)/shard_map/cokr,ckw->corw/dot_general | solution.py:65
  (2 shorter events, 0.0 us)
Async XLA Ops:
  6.5 135.9 %all-gather.2.cloned.1.call-start = ((), (), s32[]{:S(2)}) async-start(), calls=%async_computation.1 | async-start | bytes 4718592 | tf_op jit(solution)/shard_map/all_gather | solution.py:63
  15.4 21.7 %collective-permute-start = (bf16[512,1536]{0,1:T(8,128)(2,1)S(1)}, bf16[512,1536]{0,1:T(8,128)(2,1)S(1)}, u32[]{:S(2)}, u32[]{:S(2)}) collective-permute-start(bf16[512,1536]{0,1:T(8,128)(2,1)S(1)} %slice_convert_fusion), channel_id=1, source_target_pairs={{0,1},{1,4},{4,5},{5,8},{8,9},{9,12},{12,13},{2,3},{3,6},{6,7},{7,... | collective-permute-start | bytes 4718600 | tf_op jit(solution)/shard_map/ppermute | solution.py:16
Sparse Core Ops, SparseCore 0:
  95.8 46.6 all-gather.1
where the time goes:
time: 169 us; the launch traced here: 167 us
  waiting for transfers between devices  58.6 us (35%)
  blocking collectives  39.5 us (23%)
  matrix products  25 us (15%)
  local copies, waits for them, and re-layouts  15.6 us (9%)
  between operations  13.5 us (8%)
  other arithmetic  13.2 us (8%)
  starting transfers between devices  1.92 us (1%)
    all_gather x1, waiting for transfers between devices, per_device(): piece = lax.all_gather(turned, 'gy', axis=3, tiled=True)  43.6 us
    all_to_all x1, blocking collectives, per_device(): lax.all_to_all(spectra, ('gx', 'gz'), split_axis=0, concat_axis=2, tiled=...  39.5 us
    ppermute x1, waiting for transfers between devices, passed_along(): return lax.ppermute(value, axis, pairs)  14.9 us
    dot_general x1, matrix products, per_device(): jnp.einsum('cokr,ckw->corw', stacked, columns, preferred_element_type=jnp...  14.3 us
    dot_general x1, matrix products, per_device(): jnp.einsum('krn,isn->krsi', basis, frames, preferred_element_type=jnp.flo...  10.6 us
    unnamed x1, local copies, waits for them, and re-layouts  6.56 us
    concatenate x1, other arithmetic, per_device(): jnp.concatenate([earlier.astype(jnp.float32), voltages.astype(jnp.float32...  4.86 us
    all_gather x1, local copies, waits for them, and re-layouts, per_device(): piece = lax.all_gather(turned, 'gy', axis=3, tiled=True)  3.61 us
  transfers between devices with their start and end apart: 2, of which 2 were waited for; matrix products, arithmetic and copies ran while one was open for 5% of the time, Pallas kernels for 0%

commit v1 on v0

v1 whole, which is shorter than its diff:
```python
import functools
import math

import jax
import jax.numpy as jnp
import numpy as np
from jax import lax
from jax.experimental import pallas as pl
from jax.experimental.pallas import tpu as pltpu
from jax.sharding import PartitionSpec as P

CHANS = 128
POINTS = 512
TAPS = 4
LANES = 128
MESH = pl.DeviceIdType.MESH
F32 = jnp.float32
BF16 = jnp.bfloat16


def filter_taps():
    index = np.arange(TAPS * POINTS, dtype=np.float64)
    centre = (TAPS * POINTS - 1) / 2.0
    window = 0.5 - 0.5 * np.cos(2.0 * math.pi * (index + 0.5) / (TAPS * POINTS))
    taps = (np.sinc((index - centre) / POINTS) * window).astype(np.float32)
    return (taps / np.float32(128.0)).reshape(TAPS, POINTS)


def basis_rows(peers, rows_per):
    sample = np.arange(POINTS)[None, :]
    channel = 64 + np.arange(CHANS)[:, None]
    phase = (sample * channel % POINTS) * (2.0 * math.pi / POINTS)
    scale = 1.0 / math.sqrt(POINTS)
    table = np.stack([np.cos(phase) * scale, -np.sin(phase) * scale], axis=1)
    table = table.reshape(peers, -1, POINTS)
    out = np.zeros((peers, rows_per, POINTS), np.float32)
    out[:, : table.shape[1]] = table
    return out.reshape(peers * rows_per, POINTS)


def spread_kernel(
    gxn, gzn, gyn, spec, rows_per,
    v_ref, taps_ref, basis_ref, g_ref,
    frames, spectra, tail_out, tail_in,
    send_sem, recv_sem, pass_send, pass_recv, local_sem, tail_sem,
):
    peers = gxn * gzn
    inputs = v_ref.shape[0]
    x = lax.axis_index("gy")
    me = lax.axis_index("gx") * gzn + lax.axis_index("gz")

    def at(peer):
        return {"gx": peer // gzn, "gz": lax.rem(peer, gzn)}

    def across(k):
        return {"gy": lax.rem(x + k, gyn)}

    barrier = pltpu.get_barrier_semaphore()

    def greet(k, carry):
        pl.semaphore_signal(
            barrier, inc=1, device_id=at(lax.rem(me + k, peers)), device_id_type=MESH
        )
        return carry

    lax.fori_loop(1, peers, greet, 0)
    for k in range(1, gyn):
        pl.semaphore_signal(barrier, inc=1, device_id=across(k), device_id_type=MESH)

    step = 32

    def filtered(slot, terms):
        def body(chunk, carry):
            rows = pl.ds(pl.multiple_of(chunk * step, step), step)
            total = jnp.zeros((step, POINTS), F32)
            for tap, block in terms:
                piece = v_ref[rows, block * POINTS : (block + 1) * POINTS].astype(F32)
                total = total + taps_ref[tap : tap + 1, :] * piece
            frames[slot, rows, :] = total.astype(BF16)
            return carry

        lax.fori_loop(0, inputs // step, body, 0)
        return lax.dot_general(
            basis_ref[...], frames[slot], (((1,), (1,)), ((), ())), preferred_element_type=F32
        )

    def rows_of(peer, s):
        return pl.ds(pl.multiple_of((peer * spec + s) * rows_per, rows_per), rows_per)

    def owned(peer):
        return pl.ds(pl.multiple_of(peer * rows_per, rows_per), rows_per)

    def send(peer, s):
        return pltpu.make_async_remote_copy(
            src_ref=spectra.at[s, owned(peer)],
            dst_ref=g_ref.at[x, rows_of(me, s)],
            send_sem=send_sem.at[peer, s],
            recv_sem=recv_sem.at[me, s],
            device_id=at(peer),
            device_id_type=MESH,
        )

    def arrival(peer, s):
        return pltpu.make_async_remote_copy(
            src_ref=spectra.at[s, owned(peer)],
            dst_ref=g_ref.at[x, rows_of(peer, s)],
            send_sem=send_sem.at[peer, s],
            recv_sem=recv_sem.at[peer, s],
            device_id=at(peer),
            device_id_type=MESH,
        )

    def pass_on(source, peer, s, k):
        return pltpu.make_async_remote_copy(
            src_ref=source,
            dst_ref=g_ref.at[x, rows_of(peer, s)],
            send_sem=pass_send.at[k - 1, peer, s],
            recv_sem=pass_recv.at[k - 1, peer, s],
            device_id=across(k),
            device_id_type=MESH,
        )

    def passed(peer, s, k):
        y = lax.rem(x - k + gyn, gyn)
        return pltpu.make_async_remote_copy(
            src_ref=g_ref.at[y, rows_of(peer, s)],
            dst_ref=g_ref.at[y, rows_of(peer, s)],
            send_sem=pass_send.at[k - 1, peer, s],
            recv_sem=pass_recv.at[k - 1, peer, s],
            device_id=across(k),
            device_id_type=MESH,
        )

    def local(s):
        return pltpu.make_async_copy(
            spectra.at[s, owned(me)], g_ref.at[x, rows_of(me, s)], local_sem.at[s]
        )

    def tail(peer):
        return pltpu.make_async_remote_copy(
            src_ref=tail_out,
            dst_ref=tail_in,
            send_sem=tail_sem.at[0],
            recv_sem=tail_sem.at[1],
            device_id=at(peer),
            device_id_type=MESH,
        )

    for s in range(TAPS - 1):
        terms = [(t, spec + s - 3 + t) for t in range(TAPS) if s - 3 + t < 0]
        tail_out[s] = filtered(s % 2, terms).astype(BF16)

    pl.semaphore_wait(barrier, peers - 1 + gyn - 1)

    @pl.when(me < peers - 1)
    def _():
        tail(me + 1).start()

    def launch(s):
        local(s).start()
        for k in range(1, gyn):
            pass_on(spectra.at[s, owned(me)], me, s, k).start()

        def body(k, carry):
            send(lax.rem(me + peers - k, peers), s).start()
            return carry

        lax.fori_loop(1, peers, body, 0)

    order = list(range(TAPS - 1, spec)) + list(range(TAPS - 1))
    for s in order:
        terms = [(t, s - 3 + t) for t in range(TAPS) if s - 3 + t >= 0]
        found = filtered(s % 2, terms)
        if s < TAPS - 1:
            if s == 0:
                @pl.when(me > 0)
                def _():
                    tail(me - 1).wait_recv()

                @pl.when(me == 0)
                def _():
                    tail_in[...] = jnp.zeros_like(tail_in)

            found = found + tail_in[s].astype(F32)
        spectra[s] = found.astype(BF16)
        launch(s)

    for s in order:
        def body(k, carry, s=s):
            peer = lax.rem(me + k, peers)
            arrival(peer, s).wait_recv()
            for j in range(1, gyn):
                pass_on(g_ref.at[x, rows_of(peer, s)], peer, s, j).start()
            return carry

        lax.fori_loop(1, peers, body, 0)

    @pl.when(me < peers - 1)
    def _():
        tail(me + 1).wait_send()

    for s in order:
        local(s).wait()

        def body(k, carry, s=s):
            send(lax.rem(me + k, peers), s).wait_send()
            return carry

        lax.fori_loop(1, peers, body, 0)

        def body(peer, carry, s=s):
            for j in range(1, gyn):
                passed(peer, s, j).wait()
            return carry

        lax.fori_loop(0, peers, body, 0)


def correlate_kernel(gyn, times, rows_per, rows_kept, inverse, g_ref, out_ref, wide, right):
    x = lax.axis_index("gy")
    c = pl.program_id(0)
    inputs = g_ref.shape[2]
    depth = right.shape[0]

    @pl.when(c == 0)
    def _():
        right[...] = jnp.zeros_like(right)
        for y in range(gyn):
            def body(t, carry, y=y):
                source = pl.ds(pl.multiple_of(t * rows_per, rows_per), rows_per)
                target = pl.ds(pl.multiple_of(t * rows_kept, rows_kept), rows_kept)
                block = g_ref[y, source, :].astype(F32)[:rows_kept]
                for lane in range(inputs // LANES):
                    wide[y, lane, target, :] = block[:, lane * LANES : (lane + 1) * LANES]
                return carry

            lax.fori_loop(0, times, body, 0)

    def part(y, r):
        rows = pl.ds(2 * c + r, times, rows_kept)
        return jnp.concatenate(
            [wide[y, lane, rows, :] for lane in range(inputs // LANES)], axis=1
        )

    for y in range(gyn):
        real, imag = part(y, 0), part(y, 1)
        left, far = slice(y * inputs, (y + 1) * inputs), slice(
            (gyn + y) * inputs, (gyn + y + 1) * inputs
        )
        right[0:times, left] = real.astype(BF16)
        right[times : 2 * times, left] = imag.astype(BF16)
        right[0:times, far] = (-imag).astype(BF16)
        right[times : 2 * times, far] = real.astype(BF16)

    pieces = [part(x, 0), part(x, 1)]
    if depth > 2 * times:
        pieces.append(jnp.zeros((depth - 2 * times, inputs), F32))
    turned = jnp.transpose(jnp.concatenate(pieces, axis=0)).astype(BF16)
    for r in range(2):
        for y in range(gyn):
            left = slice((r * gyn + y) * inputs, (r * gyn + y + 1) * inputs)
            product = jnp.dot(turned, right[:, left], preferred_element_type=F32)
            out_ref[0, r, :, y * inputs : (y + 1) * inputs] = (product * inverse).astype(BF16)


def solution(mesh):
    gxn, gzn, gyn = mesh.shape["gx"], mesh.shape["gz"], mesh.shape["gy"]
    peers = gxn * gzn
    chans = CHANS // peers
    rows_per = -(-2 * chans // 16) * 16
    rows_kept = -(-2 * chans // 8) * 8
    taps = filter_taps()
    basis = basis_rows(peers, rows_per)

    def per_device(voltages):
        inputs = voltages.shape[0]
        spec = voltages.shape[1] // POINTS
        times = spec * peers
        vmem = pl.BlockSpec(memory_space=pltpu.VMEM)
        dma = pltpu.SemaphoreType.DMA
        gathered = pl.pallas_call(
            functools.partial(spread_kernel, gxn, gzn, gyn, spec, rows_per),
            out_shape=jax.ShapeDtypeStruct((gyn, times * rows_per, inputs), BF16),
            in_specs=[vmem] * 3,
            out_specs=pl.BlockSpec(memory_space=pl.ANY),
            scratch_shapes=[
                pltpu.VMEM((2, inputs, POINTS), BF16),
                pltpu.VMEM((spec, peers * rows_per, inputs), BF16),
                pltpu.VMEM((TAPS - 1, peers * rows_per, inputs), BF16),
                pltpu.VMEM((TAPS - 1, peers * rows_per, inputs), BF16),
                dma((peers, spec)),
                dma((peers, spec)),
                dma((gyn - 1, peers, spec)),
                dma((gyn - 1, peers, spec)),
                dma((spec,)),
                dma((2,)),
            ],
            compiler_params=pltpu.CompilerParams(
                collective_id=0, has_side_effects=True, vmem_limit_bytes=48 * 2**20
            ),
        )(voltages, jnp.asarray(taps), jnp.asarray(basis, BF16))
        depth = -(-2 * times // 128) * 128
        return pl.pallas_call(
            functools.partial(
                correlate_kernel, gyn, times, rows_per, rows_kept, 1.0 / times
            ),
            grid=(chans,),
            out_shape=jax.ShapeDtypeStruct((chans, 2, inputs, gyn * inputs), BF16),
            in_specs=[
                pl.BlockSpec(
                    (gyn, times * rows_per, inputs),
                    lambda c: (0, 0, 0),
                    pipeline_mode=pl.Buffered(1),
                )
            ],
            out_specs=pl.BlockSpec((1, 2, inputs, gyn * inputs), lambda c: (c, 0, 0, 0)),
            scratch_shapes=[
                pltpu.VMEM((gyn, inputs // LANES, times * rows_kept, LANES), F32),
                pltpu.VMEM((depth, 2 * gyn * inputs), BF16),
            ],
            compiler_params=pltpu.CompilerParams(
                dimension_semantics=("arbitrary",), vmem_limit_bytes=56 * 2**20
            ),
        )(gathered)

    return jax.shard_map(
        per_device,
        mesh=mesh,
        in_specs=(P("gy", ("grp", "gx", "gz")),),
        out_specs=P(("grp", "gx", "gz"), None, "gy", None),
        check_vma=False,
    )
```

time: 169 us -> 93.7 us (0.55)
  Pallas kernels: 0 us -> 90.2 us
  waiting for transfers between devices: 58.6 us -> 0 us
  blocking collectives: 39.5 us -> 0 us
  matrix products: 25 us -> 0 us
  between operations: 13.5 us -> 0.02 us
  other arithmetic: 13.2 us -> 0 us
  local copies, waits for them, and re-layouts: 15.6 us -> 3.29 us
  starting transfers between devices: 1.92 us -> 0 us
    pallas_call x0 -> x2, Pallas kernels: none -> 90.2 us  [the longest x1 66.5 us: per_device(): pl.pallas_call(functools.partial(spread_kernel, gxn, gzn, gyn, spec, rows...]
    all_gather x1 -> x0, waiting for transfers between devices: 43.6 us -> none  [per_device(): piece = lax.all_gather(turned, 'gy', axis=3, tiled=True)]
    all_to_all x1 -> x0, blocking collectives: 39.5 us -> none  [per_device(): lax.all_to_all(spectra, ('gx', 'gz'), split_axis=0, concat_axis=2, tiled=...]
    dot_general x2 -> x0, matrix products: 25 us -> none  [the longest x1 14.3 us: per_device(): jnp.einsum('cokr,ckw->corw', stacked, columns, preferred_element_type=jnp...]
    ppermute x1 -> x0, waiting for transfers between devices: 14.9 us -> none  [passed_along(): return lax.ppermute(value, axis, pairs)]
    concatenate x1 -> x0, other arithmetic: 4.86 us -> none  [per_device(): jnp.concatenate([earlier.astype(jnp.float32), voltages.astype(jnp.float32...]
    convert_element_type x2 -> x0, other arithmetic: 3.98 us -> none  [the longest x1 3.55 us: per_device(): voltages.astype(jnp.float32)]
    another operation x3 -> x0, other arithmetic: 3.87 us -> none
  transfers between devices with their start and end apart: 2 -> 0, of which waited for: 2 -> 0; matrix products, arithmetic and copies ran while one was open for 5% -> 0% of each run, Pallas kernels for 0% -> 0%
where the time goes in v1:
time: 93.7 us; the launch traced here: 93.5 us
  Pallas kernels  90.2 us (96%)
  local copies, waits for them, and re-layouts  3.29 us (4%)
    pallas_call x1, Pallas kernels, per_device(): pl.pallas_call(functools.partial(spread_kernel, gxn, gzn, gyn, spec, rows...  66.5 us
    pallas_call x1, Pallas kernels, per_device(): pl.pallas_call(functools.partial(correlate_kernel, gyn, times, rows_per,...  23.6 us
    unnamed x6, local copies, waits for them, and re-layouts  3.29 us

profile of v1, /device:TPU:16, one launch (start us, length us, event | category | flops | bytes accessed | tf_op | source)
XLA Modules:
  0.0 93.5 jit_solution(4852341716262052593)
XLA Ops:
  0.0 0.0 copy-start.1
  0.0 0.9 %copy-done.1 = bf16[256,512]{1,0:T(8,128)(2,1)S(1)} copy-done((bf16[256,512]{1,0:T(8,128)(2,1)S(1)}, bf16[256,512]{1,0:T(8,128)(2,1)}, u32[]{:S(2)}) %copy-start.1) | copy-done | bytes 262168
  1.0 0.0 copy-start.2
  1.0 0.7 copy-done.2
  1.6 66.5 %shard_map.37.g_ref = bf16[2,1536,512]{2,1,0:T(8,128)(2,1)S(1)} custom-call(s32[512,3072]{1,0:T(8,128)} %v_ref.1, f32[4,512]{1,0:T(4,128)S(1)} %copy-done.2, bf16[256,512]{1,0:T(8,128)(2,1)S(1)} %copy-done.1), custom_call_target="tpu_custom_call" | custom-call | tf_op jit(solution)/shard_map/pallas_call | solution.py:281
  68.2 0.0 copy-start
  68.2 1.6 %copy-done = bf16[2,1536,512]{2,1,0:T(8,128)(2,1)} copy-done((bf16[2,1536,512]{2,1,0:T(8,128)(2,1)}, bf16[2,1536,512]{2,1,0:T(8,128)(2,1)S(1)}, u32[]{:S(2)}) %copy-start) | copy-done | bytes 3145752
  69.8 23.6 %shard_map.38 = bf16[16,2,512,1024]{3,2,1,0:T(8,128)(2,1)} custom-call(bf16[2,1536,512]{2,1,0:T(8,128)(2,1)} %copy-done), custom_call_target="tpu_custom_call" | custom-call | tf_op jit(solution)/shard_map/pallas_call | solution.py:303
Async XLA Ops:
  0.0 0.9 %copy-start.1 = (bf16[256,512]{1,0:T(8,128)(2,1)S(1)}, bf16[256,512]{1,0:T(8,128)(2,1)}, u32[]{:S(2)}) copy-start(bf16[256,512]{1,0:T(8,128)(2,1)} %constant.5.clone.basis_ref) | copy-start | bytes 786436
  1.0 0.7 copy-start.2
  68.2 1.7 %copy-start = (bf16[2,1536,512]{2,1,0:T(8,128)(2,1)}, bf16[2,1536,512]{2,1,0:T(8,128)(2,1)S(1)}, u32[]{:S(2)}) copy-start(bf16[2,1536,512]{2,1,0:T(8,128)(2,1)S(1)} %shard_map.37.g_ref) | copy-start | bytes 9437188

commit v2 on v1

--- a/solution.py
+++ b/solution.py
@@ -13,6 +13,12 @@
 POINTS = 512
 TAPS = 4
 LANES = 128
+LOADS = 4
+STEP = 16
+AHEAD = 5
+CUTS = 4
+NB = 256
+PER = 2
 MESH = pl.DeviceIdType.MESH
 F32 = jnp.float32
 BF16 = jnp.bfloat16
@@ -41,7 +47,7 @@
 def spread_kernel(
     gxn, gzn, gyn, spec, rows_per,
     v_ref, taps_ref, basis_ref, g_ref,
-    frames, spectra, tail_out, tail_in,
+    samples, taps, basis, frames, spectra, tail_out, tail_in, load_sem,
     send_sem, recv_sem, pass_send, pass_recv, local_sem, tail_sem,
 ):
     peers = gxn * gzn
@@ -67,21 +73,55 @@
     for k in range(1, gyn):
         pl.semaphore_signal(barrier, inc=1, device_id=across(k), device_id_type=MESH)
 
-    step = 32
-
-    def filtered(slot, terms):
-        def body(chunk, carry):
-            rows = pl.ds(pl.multiple_of(chunk * step, step), step)
-            total = jnp.zeros((step, POINTS), F32)
-            for tap, block in terms:
-                piece = v_ref[rows, block * POINTS : (block + 1) * POINTS].astype(F32)
-                total = total + taps_ref[tap : tap + 1, :] * piece
-            frames[slot, rows, :] = total.astype(BF16)
-            return carry
-
-        lax.fori_loop(0, inputs // step, body, 0)
+    chunk = inputs // LOADS
+
+    def loading(j):
+        rows = slice(j * chunk, (j + 1) * chunk)
+        return pltpu.make_async_copy(v_ref.at[rows], samples.at[rows], load_sem.at[j])
+
+    loads = [
+        pltpu.make_async_copy(taps_ref, taps, load_sem.at[LOADS]),
+        pltpu.make_async_copy(basis_ref, basis, load_sem.at[LOADS + 1]),
+    ]
+    loads[0].start()
+    for j in range(LOADS):
+        loading(j).start()
+    loads[1].start()
+    loads[0].wait()
+
+    shares = [
+        [(t, s - 3 + t) for t in range(TAPS) if 0 <= s - 3 + t < spec]
+        for s in range(spec + TAPS - 1)
+    ]
+    for j in range(LOADS):
+        loading(j).wait()
+        for lane in range(POINTS // LANES):
+            lanes = slice(lane * LANES, (lane + 1) * LANES)
+            held = [
+                jnp.broadcast_to(taps[t : t + 1, lanes], (STEP, LANES)) for t in range(TAPS)
+            ]
+
+            def body(i, carry, j=j, lane=lane, lanes=lanes, held=held):
+                rows = pl.ds(pl.multiple_of(j * chunk + i * STEP, STEP), STEP)
+                pieces = [
+                    samples[rows, b * POINTS + lane * LANES : b * POINTS + (lane + 1) * LANES]
+                    .astype(F32)
+                    for b in range(spec)
+                ]
+                for s, terms in enumerate(shares):
+                    total = None
+                    for t, b in terms:
+                        term = held[t] * pieces[b]
+                        total = term if total is None else total + term
+                    frames[s, rows, lanes] = total.astype(BF16)
+                return carry
+
+            lax.fori_loop(0, chunk // STEP, body, 0, unroll=2)
+    loads[1].wait()
+
+    def transformed(s):
         return lax.dot_general(
-            basis_ref[...], frames[slot], (((1,), (1,)), ((), ())), preferred_element_type=F32
+            basis[...], frames[s], (((1,), (1,)), ((), ())), preferred_element_type=F32
         )
 
     def rows_of(peer, s):
@@ -136,25 +176,30 @@
             spectra.at[s, owned(me)], g_ref.at[x, rows_of(me, s)], local_sem.at[s]
         )
 
-    def tail(peer):
-        return pltpu.make_async_remote_copy(
-            src_ref=tail_out,
-            dst_ref=tail_in,
-            send_sem=tail_sem.at[0],
-            recv_sem=tail_sem.at[1],
-            device_id=at(peer),
-            device_id_type=MESH,
-        )
+    cut = tail_out.shape[1] // CUTS
+
+    def tail(peer, s):
+        return [
+            pltpu.make_async_remote_copy(
+                src_ref=tail_out.at[s, pl.ds(q * cut, cut)],
+                dst_ref=tail_in.at[s, pl.ds(q * cut, cut)],
+                send_sem=tail_sem.at[0, s, q],
+                recv_sem=tail_sem.at[1, s, q],
+                device_id=at(peer),
+                device_id_type=MESH,
+            )
+            for q in range(CUTS)
+        ]
 
     for s in range(TAPS - 1):
-        terms = [(t, spec + s - 3 + t) for t in range(TAPS) if s - 3 + t < 0]
-        tail_out[s] = filtered(s % 2, terms).astype(BF16)
-
-    pl.semaphore_wait(barrier, peers - 1 + gyn - 1)
-
-    @pl.when(me < peers - 1)
-    def _():
-        tail(me + 1).start()
+        tail_out[s] = transformed(spec + s).astype(BF16)
+        if s == 0:
+            pl.semaphore_wait(barrier, peers - 1 + gyn - 1)
+
+        @pl.when(me < peers - 1)
+        def _(s=s):
+            for copy in tail(me + 1, s):
+                copy.start()
 
     def launch(s):
         local(s).start()
@@ -167,26 +212,26 @@
 
         lax.fori_loop(1, peers, body, 0)
 
-    order = list(range(TAPS - 1, spec)) + list(range(TAPS - 1))
-    for s in order:
-        terms = [(t, s - 3 + t) for t in range(TAPS) if s - 3 + t >= 0]
-        found = filtered(s % 2, terms)
+    order = list(range(spec))
+
+    def produce(s):
+        found = transformed(s)
         if s < TAPS - 1:
-            if s == 0:
-                @pl.when(me > 0)
-                def _():
-                    tail(me - 1).wait_recv()
-
-                @pl.when(me == 0)
-                def _():
-                    tail_in[...] = jnp.zeros_like(tail_in)
+            @pl.when(me > 0)
+            def _():
+                for copy in tail(me - 1, s):
+                    copy.wait_recv()
+
+            @pl.when(me == 0)
+            def _():
+                tail_in[s] = jnp.zeros_like(tail_in[s])
 
             found = found + tail_in[s].astype(F32)
         spectra[s] = found.astype(BF16)
         launch(s)
 
-    for s in order:
-        def body(k, carry, s=s):
+    def relay(s):
+        def body(k, carry):
             peer = lax.rem(me + k, peers)
             arrival(peer, s).wait_recv()
             for j in range(1, gyn):
@@ -195,9 +240,17 @@
 
         lax.fori_loop(1, peers, body, 0)
 
+    for i in range(spec + AHEAD):
+        if i < spec:
+            produce(order[i])
+        if i >= AHEAD:
+            relay(order[i - AHEAD])
+
     @pl.when(me < peers - 1)
     def _():
-        tail(me + 1).wait_send()
+        for s in range(TAPS - 1):
+            for copy in tail(me + 1, s):
+                copy.wait_send()
 
     for s in order:
         local(s).wait()
@@ -216,11 +269,11 @@
         lax.fori_loop(0, peers, body, 0)
 
 
-def correlate_kernel(gyn, times, rows_per, rows_kept, inverse, g_ref, out_ref, wide, right):
+def correlate_kernel(gyn, times, rows_per, rows_kept, inverse, g_ref, out_ref, wide, right, turned_ref):
     x = lax.axis_index("gy")
     c = pl.program_id(0)
     inputs = g_ref.shape[2]
-    depth = right.shape[0]
+    depth = right.shape[1]
 
     @pl.when(c == 0)
     def _():
@@ -236,31 +289,37 @@
 
             lax.fori_loop(0, times, body, 0)
 
-    def part(y, r):
-        rows = pl.ds(2 * c + r, times, rows_kept)
-        return jnp.concatenate(
-            [wide[y, lane, rows, :] for lane in range(inputs // LANES)], axis=1
-        )
-
-    for y in range(gyn):
-        real, imag = part(y, 0), part(y, 1)
-        left, far = slice(y * inputs, (y + 1) * inputs), slice(
-            (gyn + y) * inputs, (gyn + y + 1) * inputs
-        )
-        right[0:times, left] = real.astype(BF16)
-        right[times : 2 * times, left] = imag.astype(BF16)
-        right[0:times, far] = (-imag).astype(BF16)
-        right[times : 2 * times, far] = real.astype(BF16)
-
-    pieces = [part(x, 0), part(x, 1)]
-    if depth > 2 * times:
-        pieces.append(jnp.zeros((depth - 2 * times, inputs), F32))
-    turned = jnp.transpose(jnp.concatenate(pieces, axis=0)).astype(BF16)
-    for r in range(2):
+    def prepare(h):
+        def part(y, r):
+            rows = pl.ds(2 * (PER * c + h) + r, times, rows_kept)
+            return jnp.concatenate(
+                [wide[y, lane, rows, :] for lane in range(inputs // LANES)], axis=1
+            )
+
         for y in range(gyn):
-            left = slice((r * gyn + y) * inputs, (r * gyn + y + 1) * inputs)
-            product = jnp.dot(turned, right[:, left], preferred_element_type=F32)
-            out_ref[0, r, :, y * inputs : (y + 1) * inputs] = (product * inverse).astype(BF16)
+            columns = slice(y * inputs, (y + 1) * inputs)
+            right[h, 0:times, columns] = part(y, 0).astype(BF16)
+            right[h, times : 2 * times, columns] = part(y, 1).astype(BF16)
+
+        real, imag = part(x, 0), part(x, 1)
+        rest = [jnp.zeros((depth - 2 * times, inputs), F32)] if depth > 2 * times else []
+        for r, pieces in enumerate(([real, imag], [imag, -real])):
+            turned = jnp.transpose(jnp.concatenate(pieces + rest, axis=0))
+            turned_ref[h, r * inputs : (r + 1) * inputs, :] = turned.astype(BF16)
+
+    def multiply(h):
+        wide_n = min(NB, inputs)
+        for col in range(0, gyn * inputs, wide_n):
+            columns = slice(col, col + wide_n)
+            product = jnp.dot(turned_ref[h], right[h, :, columns], preferred_element_type=F32)
+            product = (product * inverse).astype(BF16)
+            for r in range(2):
+                out_ref[h, r, :, columns] = product[r * inputs : (r + 1) * inputs]
+
+    for h in range(PER):
+        prepare(h)
+    for h in range(PER):
+        multiply(h)
 
 
 def solution(mesh):
@@ -272,39 +331,45 @@
     taps = filter_taps()
     basis = basis_rows(peers, rows_per)
 
-    def per_device(voltages):
+    def spread(voltages):
         inputs = voltages.shape[0]
         spec = voltages.shape[1] // POINTS
         times = spec * peers
-        vmem = pl.BlockSpec(memory_space=pltpu.VMEM)
         dma = pltpu.SemaphoreType.DMA
-        gathered = pl.pallas_call(
+        return pl.pallas_call(
             functools.partial(spread_kernel, gxn, gzn, gyn, spec, rows_per),
             out_shape=jax.ShapeDtypeStruct((gyn, times * rows_per, inputs), BF16),
-            in_specs=[vmem] * 3,
-            out_specs=pl.BlockSpec(memory_space=pl.ANY),
+            in_specs=[pl.BlockSpec(memory_space=pl.ANY)] * 3,
+            out_specs=pl.BlockSpec(memory_space=pltpu.VMEM),
             scratch_shapes=[
-                pltpu.VMEM((2, inputs, POINTS), BF16),
+                pltpu.VMEM(voltages.shape, jnp.int32),
+                pltpu.VMEM(taps.shape, F32),
+                pltpu.VMEM(basis.shape, BF16),
+                pltpu.VMEM((spec + TAPS - 1, inputs, POINTS), BF16),
                 pltpu.VMEM((spec, peers * rows_per, inputs), BF16),
                 pltpu.VMEM((TAPS - 1, peers * rows_per, inputs), BF16),
                 pltpu.VMEM((TAPS - 1, peers * rows_per, inputs), BF16),
+                dma((LOADS + 2,)),
                 dma((peers, spec)),
                 dma((peers, spec)),
                 dma((gyn - 1, peers, spec)),
                 dma((gyn - 1, peers, spec)),
                 dma((spec,)),
-                dma((2,)),
+                dma((2, TAPS - 1, CUTS)),
             ],
             compiler_params=pltpu.CompilerParams(
-                collective_id=0, has_side_effects=True, vmem_limit_bytes=48 * 2**20
+                collective_id=0, has_side_effects=True, vmem_limit_bytes=60 * 2**20
             ),
         )(voltages, jnp.asarray(taps), jnp.asarray(basis, BF16))
+
+    def correlate(gathered):
+        inputs, times = gathered.shape[2], gathered.shape[1] // rows_per
         depth = -(-2 * times // 128) * 128
         return pl.pallas_call(
             functools.partial(
                 correlate_kernel, gyn, times, rows_per, rows_kept, 1.0 / times
             ),
-            grid=(chans,),
+            grid=(chans // PER,),
             out_shape=jax.ShapeDtypeStruct((chans, 2, inputs, gyn * inputs), BF16),
             in_specs=[
                 pl.BlockSpec(
@@ -313,15 +378,19 @@
                     pipeline_mode=pl.Buffered(1),
                 )
             ],
-            out_specs=pl.BlockSpec((1, 2, inputs, gyn * inputs), lambda c: (c, 0, 0, 0)),
+            out_specs=pl.BlockSpec((PER, 2, inputs, gyn * inputs), lambda c: (c, 0, 0, 0)),
             scratch_shapes=[
                 pltpu.VMEM((gyn, inputs // LANES, times * rows_kept, LANES), F32),
-                pltpu.VMEM((depth, 2 * gyn * inputs), BF16),
+                pltpu.VMEM((PER, depth, gyn * inputs), BF16),
+                pltpu.VMEM((PER, 2 * inputs, depth), BF16),
             ],
             compiler_params=pltpu.CompilerParams(
-                dimension_semantics=("arbitrary",), vmem_limit_bytes=56 * 2**20
+                dimension_semantics=("arbitrary",), vmem_limit_bytes=60 * 2**20
             ),
         )(gathered)
+
+    def per_device(voltages):
+        return correlate(spread(voltages))
 
     return jax.shard_map(
         per_device,

time: 93.7 us -> 85.7 us (0.915)
  Pallas kernels: 90.2 us -> 84.9 us
  local copies, waits for them, and re-layouts: 3.29 us -> 0 us
    pallas_call x2, Pallas kernels: 90.2 us -> 84.9 us  [the longest x1 64.5 us: spread(): pl.pallas_call(functools.partial(spread_kernel, gxn, gzn, gyn, spec, rows...]
    unnamed x6 -> x0, local copies, waits for them, and re-layouts: 3.29 us -> none
where the time goes in v2:
time: 85.7 us; the launch traced here: 84.9 us
  Pallas kernels  84.9 us (99%)
    pallas_call x1, Pallas kernels, spread(): pl.pallas_call(functools.partial(spread_kernel, gxn, gzn, gyn, spec, rows...  64.5 us
    pallas_call x1, Pallas kernels, correlate(): pl.pallas_call(functools.partial(correlate_kernel, gyn, times, rows_per,...  20.4 us

profile of v2, /device:TPU:16, one launch (start us, length us, event | category | flops | bytes accessed | tf_op | source)
XLA Modules:
  0.0 84.9 jit_solution(13021951163420129885)
XLA Ops:
  0.0 64.5 %shard_map.37.g_ref = bf16[2,1536,512]{2,1,0:T(8,128)(2,1)} custom-call(s32[512,3072]{1,0:T(8,128)} %v_ref.1, f32[4,512]{1,0:T(4,128)} %constant.4.clone.taps_ref, bf16[256,512]{1,0:T(8,128)(2,1)} %constant.5.clone.basis_ref), custom_call_target="tpu_custom_call" | custom-call | tf_op jit(solution)/shard_map/pallas_call | solution.py:339
  64.5 20.4 %shard_map.38 = bf16[16,2,512,1024]{3,2,1,0:T(8,128)(2,1)} custom-call(bf16[2,1536,512]{2,1,0:T(8,128)(2,1)} %shard_map.37.g_ref), custom_call_target="tpu_custom_call" | custom-call | tf_op jit(solution)/shard_map/pallas_call | solution.py:368
